TPU v7x, 32 devices: a whole 2x2x4 slice. The times are simulated.
32 devices in a mesh: dp: 16 (over z, y, x), feat: 2 (over core).
Axes of the slice: x: 2, y: 2, z: 4, core: 2. Of those that a mesh axis runs over, the one named last changes fastest.
Arguments:
- inputs: float32 [20480, 640], P('dp', 'feat'), may hold values from -6 to 6
- encoder: bfloat16 [20480, 640], P('dp', 'feat'), may hold values from -6 to 6
- output_grad: float32 [20480, 640], P('dp', 'feat'), may hold values from -6 to 6
- target_lengths: int32 [32, 24], P(('dp', 'feat')), may hold values from 0 to 256, as said below
- source_lengths: int32 [32, 24], P(('dp', 'feat')), may hold values from 0 to 256, as said below
- gains: float32 [3, 640], P(None, 'feat'), may hold values from 0.5 to 1.5
- shifts: float32 [3, 640], P(None, 'feat'), may hold values from -2 to 2
- self_inproj: bfloat16 [640, 1920], replicated, may hold values from -0.25 to 0.25
- self_outproj: bfloat16 [640, 640], replicated, may hold values from -1 to 1
- cross_query: bfloat16 [640, 640], replicated, may hold values from -0.25 to 0.25
- cross_keyvalue: bfloat16 [640, 1280], replicated, may hold values from -0.25 to 0.25
- cross_outproj: bfloat16 [640, 640], replicated, may hold values from -1 to 1
- ffn_expand: bfloat16 [640, 3072], replicated, may hold values from -0.25 to 0.25
- ffn_reduce: bfloat16 [3072, 640], replicated, may hold values from -0.109375 to 0.109375
Outputs:
- layer_out: float32 [20480, 640], P('dp', 'feat')
- input_grad: float32 [20480, 640], P('dp', 'feat')
- encoder_grad: float32 [20480, 640], P('dp', 'feat')
- gain_grad: float32 [3, 640], P(None, 'feat')
- shift_grad: float32 [3, 640], P(None, 'feat')
- self_inproj_grad: float32 [640, 1920], P('dp', 'feat')
- self_outproj_grad: float32 [640, 640], P('dp', 'feat')
- cross_query_grad: float32 [640, 640], P('dp', 'feat')
- cross_keyvalue_grad: float32 [640, 1280], P('dp', 'feat')
- cross_outproj_grad: float32 [640, 640], P('dp', 'feat')
- ffn_expand_grad: float32 [640, 3072], P('dp', 'feat')
- ffn_reduce_grad: float32 [3072, 640], P('dp', 'feat')
Inputs may be any that keep to these rules, and one draw needn't show every extreme that they name: `target_lengths`: in each bucket the nonzero lengths fill the first slots and zeros the rest; a bucket's lengths sum to 640 or less; in every draw one bucket, chosen from the seed, has a first sentence of 256. `source_lengths`: nonzero exactly where target_lengths is, and at most the target length.
All inputs are finite; a program needn't handle non-finite values.
Results may differ from a plain program's by a relative error of at most 0.017.
Values may be sent and summed in bfloat16 or wider, within the bound.
A program may use at most 192 MiB of HBM per device.

v0:
```python
import math
import jax
import jax.numpy as jnp
from jax import lax
from jax.sharding import PartitionSpec as P

HEADS = 8
EPSILON = 1e-05
MASKED_SCORE = -1e30


def as_sent(array):

    def short(part):
        return part.astype(jnp.bfloat16) if part.dtype == jnp.float32 else part

    return jax.tree.map(short, array)


def inner(left, right):
    return lax.dot_general(
        left, right, (((0,), (0,)), ((), ())), preferred_element_type=jnp.float32
    )


def backward_product(grad, weight):
    return lax.dot_general(
        grad, weight, (((1,), (1,)), ((), ())), preferred_element_type=jnp.float32
    )


def smooth_gate(values):
    return jax.nn.gelu(values, approximate=True)


def row_sums(first, second):
    return (first, second)


def to_tokens(parts):
    return parts


def to_features(parts):
    return parts


def gather_rows(part):
    return lax.all_to_all(part, "feat", split_axis=0, concat_axis=1, tiled=True)


def spread_rows(part):
    return lax.all_to_all(part, "feat", split_axis=1, concat_axis=0, tiled=True)


def norm_forward(values, gain, shift):
    width = values.shape[1]
    total, squares = row_sums(jnp.sum(values, axis=1), jnp.sum(values * values, axis=1))
    center = total / width
    reciprocal = lax.rsqrt(squares / width - center * center + EPSILON)
    normed = (values - center[:, None]) * reciprocal[:, None]
    return (normed, reciprocal, (normed * gain + shift).astype(jnp.bfloat16))


def norm_backward(grad_normed, normed, reciprocal, gain):
    width = normed.shape[1]
    grad_value = grad_normed.astype(jnp.float32)
    scaled = grad_value * gain
    first, second = row_sums(jnp.sum(scaled, axis=1), jnp.sum(scaled * normed, axis=1))
    grad_input = reciprocal[:, None] * (
        scaled - first[:, None] / width - normed * (second[:, None] / width)
    )
    return (grad_input, jnp.sum(grad_value * normed, axis=0), jnp.sum(grad_value, axis=0))


def sentence_rows(lengths, count):
    slots = jnp.arange(lengths.shape[1], dtype=jnp.int32)
    ends = jnp.sum(
        jnp.where(slots[:, None] <= slots[None, :], lengths[0][:, None], 0), axis=0, dtype=jnp.int32
    )
    positions = jnp.arange(count, dtype=jnp.int32)
    sentence = jnp.sum(
        (ends[None, :] <= positions[:, None]).astype(jnp.int32), axis=1, dtype=jnp.int32
    )
    return (sentence, positions < ends[-1])


def split_heads(values):
    return values.reshape(values.shape[0], HEADS, values.shape[1] // HEADS)


def head_scores(queries, keys, allowed):
    head_size = queries.shape[1] // HEADS
    scores = jnp.einsum(
        "qhd,khd->hqk", split_heads(queries), split_heads(keys), preferred_element_type=jnp.float32
    ) * (1.0 / math.sqrt(head_size))
    return jnp.where(allowed[None, :, :], scores, MASKED_SCORE)


def attend_forward(queries, keys, values, allowed):
    scores = head_scores(queries, keys, allowed)
    largest = jnp.max(scores, axis=-1, keepdims=True)
    expo = jnp.exp(scores - largest)
    total = jnp.sum(expo, axis=-1, keepdims=True)
    weights = expo / total
    mixed = jnp.einsum(
        "hqk,khd->qhd",
        weights.astype(jnp.bfloat16),
        split_heads(values),
        preferred_element_type=jnp.float32,
    )
    log_total = largest[..., 0] + jnp.log(total[..., 0])
    return (mixed.reshape(queries.shape).astype(jnp.bfloat16), log_total)


def attend_backward(queries, keys, values, allowed, log_total, grad_mixed):
    head_size = queries.shape[1] // HEADS
    scale = 1.0 / math.sqrt(head_size)
    weights = jnp.exp(head_scores(queries, keys, allowed) - log_total[..., None])
    grad_heads = split_heads(grad_mixed)
    grad_weights = jnp.einsum(
        "qhd,khd->hqk", grad_heads, split_heads(values), preferred_element_type=jnp.float32
    )
    grad_values = jnp.einsum(
        "hqk,qhd->khd", weights.astype(jnp.bfloat16), grad_heads, preferred_element_type=jnp.float32
    )
    centre = jnp.sum(weights * grad_weights, axis=-1, keepdims=True)
    grad_scores = (weights * (grad_weights - centre)).astype(jnp.bfloat16)
    grad_queries = (
        jnp.einsum(
            "hqk,khd->qhd", grad_scores, split_heads(keys), preferred_element_type=jnp.float32
        )
        * scale
    )
    grad_keys = (
        jnp.einsum(
            "hqk,qhd->khd", grad_scores, split_heads(queries), preferred_element_type=jnp.float32
        )
        * scale
    )
    return (
        grad_queries.reshape(queries.shape),
        grad_keys.reshape(keys.shape),
        grad_values.reshape(values.shape),
    )


def masked_rows(grad, valid):
    return jnp.where(valid[:, None], grad, jnp.zeros_like(grad))


def per_device(
    inputs,
    encoder,
    output_grad,
    target_lengths,
    source_lengths,
    gains,
    shifts,
    self_inproj,
    self_outproj,
    cross_query,
    cross_keyvalue,
    cross_outproj,
    ffn_expand,
    ffn_reduce,
):
    inputs = gather_rows(inputs)
    encoder = gather_rows(encoder)
    output_grad = gather_rows(output_grad)
    gains = lax.all_gather(gains, "feat", axis=1, tiled=True)
    shifts = lax.all_gather(shifts, "feat", axis=1, tiled=True)
    count = inputs.shape[0]
    width = self_outproj.shape[0]
    target_seg, target_valid = sentence_rows(target_lengths, count)
    source_seg, source_valid = sentence_rows(source_lengths, count)
    positions = jnp.arange(count, dtype=jnp.int32)
    keep = target_valid.astype(jnp.float32)[:, None]
    self_mask = (target_seg[:, None] == target_seg[None, :]) & (
        positions[None, :] <= positions[:, None]
    )
    self_mask = self_mask & target_valid[:, None] & target_valid[None, :]
    cross_mask = (
        (target_seg[:, None] == source_seg[None, :]) & target_valid[:, None] & source_valid[None, :]
    )
    normed_one, recip_one, normed_cols = norm_forward(inputs, gains[0], shifts[0])
    (normed1,) = to_tokens((normed_cols,))
    projected = jnp.dot(normed1, self_inproj, preferred_element_type=jnp.float32).astype(
        jnp.bfloat16
    )
    queries = projected[:, :width]
    keys = projected[:, width : 2 * width]
    values = projected[:, 2 * width :]
    attended1, log_one = attend_forward(queries, keys, values, self_mask)
    branch = (jnp.dot(attended1, self_outproj, preferred_element_type=jnp.float32) * keep).astype(
        jnp.bfloat16
    )
    (branch_cols,) = to_features((branch,))
    mid_one = inputs + branch_cols.astype(jnp.float32)
    normed_two, recip_two, normed_cols = norm_forward(mid_one, gains[1], shifts[1])
    normed2, source_rows = to_tokens((normed_cols, encoder))
    cross_queries = jnp.dot(normed2, cross_query, preferred_element_type=jnp.float32).astype(
        jnp.bfloat16
    )
    memory = jnp.dot(source_rows, cross_keyvalue, preferred_element_type=jnp.float32).astype(
        jnp.bfloat16
    )
    attended2, log_two = attend_forward(
        cross_queries, memory[:, :width], memory[:, width:], cross_mask
    )
    branch = (jnp.dot(attended2, cross_outproj, preferred_element_type=jnp.float32) * keep).astype(
        jnp.bfloat16
    )
    (branch_cols,) = to_features((branch,))
    mid_two = mid_one + branch_cols.astype(jnp.float32)
    normed_three, recip_three, normed_cols = norm_forward(mid_two, gains[2], shifts[2])
    (normed3,) = to_tokens((normed_cols,))
    expanded = jnp.dot(normed3, ffn_expand, preferred_element_type=jnp.float32).astype(jnp.bfloat16)
    gated, gate_pull = jax.vjp(smooth_gate, expanded.astype(jnp.float32))
    activated = gated.astype(jnp.bfloat16)
    branch = (jnp.dot(activated, ffn_reduce, preferred_element_type=jnp.float32) * keep).astype(
        jnp.bfloat16
    )
    (branch_cols,) = to_features((branch,))
    layer_out = mid_two + branch_cols.astype(jnp.float32)
    (grad_branch,) = to_tokens((output_grad.astype(jnp.bfloat16),))
    grad_branch = masked_rows(grad_branch, target_valid)
    reduce_grad = inner(activated, grad_branch)
    grad_act = backward_product(grad_branch, ffn_reduce)
    (grad_pre,) = gate_pull(grad_act)
    grad_expanded = grad_pre.astype(jnp.bfloat16)
    expand_grad = inner(normed3, grad_expanded)
    grad_normed = backward_product(grad_expanded, ffn_expand).astype(jnp.bfloat16)
    (grad_cols,) = to_features((grad_normed,))
    part_three, gain_three, shift_three = norm_backward(
        grad_cols, normed_three, recip_three, gains[2]
    )
    grad_mid_two = output_grad + part_three
    (grad_branch,) = to_tokens((grad_mid_two.astype(jnp.bfloat16),))
    grad_branch = masked_rows(grad_branch, target_valid)
    cross_out_grad = inner(attended2, grad_branch)
    grad_attended = backward_product(grad_branch, cross_outproj).astype(jnp.bfloat16)
    grad_cq, grad_ck, grad_cv = attend_backward(
        cross_queries, memory[:, :width], memory[:, width:], cross_mask, log_two, grad_attended
    )
    grad_cq = grad_cq.astype(jnp.bfloat16)
    grad_memory = jnp.concatenate([grad_ck, grad_cv], axis=1).astype(jnp.bfloat16)
    cross_query_grad = inner(normed2, grad_cq)
    cross_kv_grad = inner(source_rows, grad_memory)
    grad_normed = backward_product(grad_cq, cross_query).astype(jnp.bfloat16)
    grad_source = backward_product(grad_memory, cross_keyvalue).astype(jnp.bfloat16)
    grad_cols, grad_source_cols = to_features((grad_normed, grad_source))
    part_two, gain_two, shift_two = norm_backward(grad_cols, normed_two, recip_two, gains[1])
    grad_mid_one = grad_mid_two + part_two
    (grad_branch,) = to_tokens((grad_mid_one.astype(jnp.bfloat16),))
    grad_branch = masked_rows(grad_branch, target_valid)
    self_out_grad = inner(attended1, grad_branch)
    grad_attended = backward_product(grad_branch, self_outproj).astype(jnp.bfloat16)
    grad_q, grad_k, grad_v = attend_backward(
        queries, keys, values, self_mask, log_one, grad_attended
    )
    grad_projected = jnp.concatenate([grad_q, grad_k, grad_v], axis=1).astype(jnp.bfloat16)
    self_in_grad = inner(normed1, grad_projected)
    grad_normed = backward_product(grad_projected, self_inproj).astype(jnp.bfloat16)
    (grad_cols,) = to_features((grad_normed,))
    part_one, gain_one, shift_one = norm_backward(grad_cols, normed_one, recip_one, gains[0])
    input_grad = grad_mid_one + part_one
    gain_local = jnp.stack([gain_one, gain_two, gain_three], axis=0)
    shift_local = jnp.stack([shift_one, shift_two, shift_three], axis=0)
    vectors = lax.psum(jnp.concatenate([gain_local, shift_local], axis=0), ("dp", "feat"))
    half = vectors.shape[1] // lax.axis_size("feat")
    vectors = lax.dynamic_slice_in_dim(vectors, lax.axis_index("feat") * half, half, axis=1)
    gain_grad, shift_grad = (vectors[:3], vectors[3:])
    weight_terms = (
        self_in_grad,
        self_out_grad,
        cross_query_grad,
        cross_kv_grad,
        cross_out_grad,
        expand_grad,
        reduce_grad,
    )
    summed = []
    for term in weight_terms:
        pair = lax.psum_scatter(term.astype(jnp.bfloat16), "feat", scatter_dimension=1, tiled=True)
        summed.append(
            lax.psum_scatter(pair, "dp", scatter_dimension=0, tiled=True).astype(jnp.float32)
        )
    return (
        spread_rows(layer_out),
        spread_rows(input_grad),
        spread_rows(grad_source_cols).astype(jnp.float32),
        gain_grad,
        shift_grad,
        *summed,
    )


def solution(mesh):
    in_specs = (
        P("dp", "feat"),
        P("dp", "feat"),
        P("dp", "feat"),
        P(("dp", "feat"), None),
        P(("dp", "feat"), None),
        P(None, "feat"),
        P(None, "feat"),
        P(),
        P(),
        P(),
        P(),
        P(),
        P(),
        P(),
    )
    out_specs = (
        P("dp", "feat"),
        P("dp", "feat"),
        P("dp", "feat"),
        P(None, "feat"),
        P(None, "feat"),
        P("dp", "feat"),
        P("dp", "feat"),
        P("dp", "feat"),
        P("dp", "feat"),
        P("dp", "feat"),
        P("dp", "feat"),
        P("dp", "feat"),
    )
    return jax.shard_map(
        per_device, mesh=mesh, in_specs=in_specs, out_specs=out_specs, check_vma=False
    )
```

profile of v0, /device:TPU:0, one launch (start us, length us, event | category | flops | bytes accessed | tf_op | source)
XLA Modules:
  0.0 732.3 jit_solution(13034640641992369800)
XLA Ops:
  23.2 4.7 all-to-all-start
  38.0 4.7 all-to-all-start.3
  58.6 8.8 %fusion.79 = f32[640,3072]{1,0:T(8,128)} fusion(bf16[640,640]{0,1:T(8,128)(2,1)S(1)} %fusion.60, bf16[3072,640]{1,0:T(8,128)(2,1)} %param.27), kind=kOutput, calls=%fused_computation.178 | convolution fusion | flops 2516582400 | bytes 12615680 | tf_op jit(solution)/shard_map/dot_general | solution.py:27
  97.4 12.5 %fusion.7 = (bf16[640,3072]{1,0:T(8,128)(2,1)S(1)}, bf16[640,3072]{1,0:T(8,128)(2,1)}) fusion(f32[640,3072]{1,0:T(8,128)} %fusion.79, bf16[640,3072]{1,0:T(8,128)(2,1)S(1)} %copy-done.50, f32[640,640]{0,1:T(8,128)S(1)} %get-tuple-element.118, f32[640]{0:T(1024)S(1)} %get-tuple-element.91, f32[640]{0:T(1024)S(1)} %get-tuple-element.130, ...), kind=kOutput, calls=%fused_computation.24 | convolution fusion | flops 2561884160 | bytes 21309440 | tf_op jit(solution)/shard_map/dot_general | solution.py:218
  121.3 12.5 %multiply_reduce_fusion.1 = (f32[8,640]{1,0:T(8,128)S(1)}, f32[8,640,640]{1,2,0:T(8,128)}) fusion(f32[8,640,640]{1,2,0:T(8,128)} %copy-done.2, f32[8,640]{1,0:T(8,128)S(1)} %log_add_fusion.1, bf16[640,8,80]{0,2,1:T(8,128)(2,1)S(1)} %bitcast.172, bf16[640,8,80]{0,2,1:T(8,128)(2,1)} %bitcast.186), kind=kOutput, calls=%fused_computation.9 | convolution fusion | flops 534113280 | bytes 27893760 | tf_op jit(solution)/shard_map/qhd,khd->hqk/dot_general | solution.py:121
  133.8 6.6 multiply_convert_fusion.1
  153.2 5.6 multiply_convert_fusion.2
  158.8 7.3 fusion.52
  172.5 12.1 %multiply_reduce_fusion = (f32[8,640]{1,0:T(8,128)S(1)}, f32[8,640,640]{1,2,0:T(8,128)}) fusion(f32[8,640,640]{1,2,0:T(8,128)} %copy-done.1, f32[8,640]{1,0:T(8,128)S(1)} %log_add_fusion, bf16[640,8,80]{0,2,1:T(8,128)(2,1)S(1)} %bitcast.174, bf16[640,8,80]{0,2,1:T(8,128)(2,1)S(1)} %bitcast.184), kind=kOutput, calls=%fused_computation.6 | convolution fusion | flops 534113280 | bytes 27893760 | tf_op jit(solution)/shard_map/qhd,khd->hqk/dot_general | solution.py:121
  185.6 6.6 multiply_convert_fusion
  204.0 7.4 %convolution_convert_fusion = bf16[3072,640]{0,1:T(8,128)(2,1)} fusion(bf16[640,640]{0,1:T(8,128)(2,1)S(1)} %copy-done.34, bf16[640,3072]{1,0:T(8,128)(2,1)} %get-tuple-element.120), kind=kOutput, calls=%fused_computation.37 | convolution fusion | flops 2538209280 | bytes 8683520 | tf_op jit(solution)/shard_map/dot_general | solution.py:21
  211.5 8.4 %convolution_convert_fusion.1 = bf16[640,3072]{1,0:T(8,128)(2,1)} fusion(bf16[640,3072]{1,0:T(8,128)(2,1)} %copy-done.55, f32[640,640]{0,1:T(8,128)} %copy-done.18, f32[640]{0:T(1024)S(1)} %get-tuple-element.91, f32[640]{0:T(1024)S(1)} %get-tuple-element.130, f32[640]{0:T(1024)S(1)} %get-tuple-element.108, f32[640]{0:T(1024)S(1)} %get-tuple-element.107), kind=kOutput, calls=%fused_computation.38 | convolution fusion | flops 2520596480 | bytes 9512960 | tf_op jit(solution)/shard_map/dot_general | solution.py:21
  223.4 8.2 %reduce-scatter.33.cloned.1.call-done = bf16[3072,320]{0,1:T(8,128)(2,1)} async-done(((bf16[3072,640]{0,1:T(8,128)(2,1)}), bf16[3072,320]{0,1:T(8,128)(2,1)}) %reduce-scatter.33.cloned.1.call-update) | async-done | bytes 1966096 | tf_op jit(solution)/shard_map/reduce_scatter | solution.py:285
  231.6 4.1 copy.180
  235.8 11.1 %reduce-scatter.29.cloned.1.call-done = bf16[640,1536]{1,0:T(8,128)(2,1)} async-done(((bf16[640,3072]{1,0:T(8,128)(2,1)}), bf16[640,1536]{1,0:T(8,128)(2,1)}) %reduce-scatter.29.cloned.1.call-update) | async-done | bytes 1966096 | tf_op jit(solution)/shard_map/reduce_scatter | solution.py:285
  246.9 8.8 %convert_add_fusion.1 = f32[640,640]{0,1:T(8,128)} fusion(f32[640,640]{0,1:T(8,128)} %copy-done.18, bf16[3072,640]{1,0:T(8,128)(2,1)} %param.27, f32[640]{0:T(1024)S(1)} %fusion.61, bf16[640,3072]{1,0:T(8,128)(2,1)} %get-tuple-element.120), kind=kOutput, calls=%fused_computation.93 | convolution fusion | flops 2537881600 | bytes 11143680 | tf_op jit(solution)/shard_map/dot_general | solution.py:221
  255.8 4.8 all-to-all-start.2
  260.6 4.1 convolution_convert_fusion.7
  278.9 4.7 all-to-all-start.4
  290.2 40.8 %psum.7 = f32[6,640]{1,0:T(8,128)S(1)} all-reduce(f32[6,640]{1,0:T(8,128)S(1)} %concatenate.13), channel_id=1, replica_groups=mesh['dp'=16,'feat'=2] {'dp','feat'}, use_global_device_ids=true, to_apply=%region_28.29 | all-reduce | flops 3840 | bytes 30720 | tf_op jit(solution)/shard_map/psum | solution.py:270
  331.7 50.3 %all-reduce.7.cloned.1.call-done = (bf16[640,320]{0,1:T(8,128)(2,1)}, bf16[640,320]{0,1:T(8,128)(2,1)}, bf16[640,640]{0,1:T(8,128)(2,1)}, bf16[640,320]{0,1:T(8,128)(2,1)}) async-done(((bf16[640,320]{0,1:T(8,128)(2,1)}, bf16[640,320]{0,1:T(8,128)(2,1)}, bf16[640,640]{0,1:T(8,128)(2,1)}, bf16[640,320]{0,1:T(8,128)(2,1)}), (bf16[640,320]{0,1:T(8,128)(2,1)}, bf16[640,320]{0,1:T(8,128)(2,1)}, ...) | async-done | bytes 2048016
  389.1 73.2 %reduce-scatter.35.cloned.1.call-done = bf16[40,960]{1,0:T(8,128)(2,1)} async-done(((bf16[640,960]{1,0:T(8,128)(2,1)}), bf16[40,960]{1,0:T(8,128)(2,1)}) %reduce-scatter.35.cloned.1.call-update) | async-done | bytes 76816
  464.1 127.7 %reduce-scatter.37.cloned.1.call-done = bf16[192,320]{1,0:T(8,128)(2,1)} async-done(((bf16[3072,320]{1,0:T(8,128)(2,1)}), bf16[192,320]{1,0:T(8,128)(2,1)}) %reduce-scatter.37.cloned.1.call-update) | async-done | bytes 122896
  593.7 129.9 %reduce-scatter.31.cloned.1.call-done = bf16[40,1536]{1,0:T(8,128)(2,1)} async-done(((bf16[640,1536]{1,0:T(8,128)(2,1)}), bf16[40,1536]{1,0:T(8,128)(2,1)}) %reduce-scatter.31.cloned.1.call-update) | async-done | bytes 122896 | tf_op jit(solution)/shard_map/reduce_scatter | solution.py:287
  (261 shorter events, 151.4 us)
Async XLA Ops:
  7.2 40.5 %copy-start = (bf16[640,1920]{1,0:T(8,128)(2,1)S(1)}, bf16[640,1920]{1,0:T(8,128)(2,1)}, u32[]{:S(2)}) copy-start(bf16[640,1920]{1,0:T(8,128)(2,1)} %param.21) | copy-start | bytes 7372804
  9.5 13.7 %all-to-all-start.1 = ((bf16[2,640,320]{1,2,0:T(8,128)(2,1)}), bf16[2,640,320]{1,2,0:T(8,128)(2,1)S(1)}, u32[]{:S(2)}, u32[]{:S(2)}) async-start(bf16[2,640,320]{1,2,0:T(8,128)(2,1)} %bitcast.161), calls=%async_computation.1 | async-start | bytes 1638400 | tf_op jit(solution)/shard_map/all_to_all | solution.py:49
  23.2 14.9 %all-to-all-start = ((f32[2,640,320]{1,2,0:T(8,128)}), f32[2,640,320]{1,2,0:T(8,128)}, u32[]{:S(2)}, u32[]{:S(2)}) async-start(f32[2,640,320]{1,2,0:T(8,128)} %bitcast.177), calls=%async_computation | async-start | bytes 3276800 | tf_op jit(solution)/shard_map/all_to_all | solution.py:49
  38.0 19.0 %all-to-all-start.3 = ((f32[2,640,320]{1,2,0:T(8,128)}), f32[2,640,320]{1,2,0:T(8,128)}, u32[]{:S(2)}, u32[]{:S(2)}) async-start(f32[2,640,320]{1,2,0:T(8,128)} %bitcast.176), calls=%async_computation.3 | async-start | bytes 3276800 | tf_op jit(solution)/shard_map/all_to_all | solution.py:49
  42.7 177.3 %reduce-scatter.27.cloned.1.call-start = ((), (), s32[]{:S(2)}) async-start(), calls=%async_computation.20 | async-start | bytes 1228800 | tf_op jit(solution)/shard_map/reduce_scatter | solution.py:285
  96.4 17.2 %copy-start.18 = (f32[640,640]{0,1:T(8,128)}, f32[640,640]{0,1:T(8,128)S(1)}, u32[]{:S(2)}) copy-start(f32[640,640]{0,1:T(8,128)S(1)} %get-tuple-element.118) | copy-start | bytes 4915204
  118.6 101.5 %reduce-scatter.23.cloned.1.call-start = ((), (), s32[]{:S(2)}) async-start(), calls=%async_computation.18 | async-start | bytes 1228800 | tf_op jit(solution)/shard_map/reduce_scatter | solution.py:285
  121.2 12.6 %slice-start.4 = ((s8[13107200]{0:T(1024)(128)(4,1)}), s8[4194304]{0:T(1024)(128)(4,1)S(1)}, s32[]{:S(2)}) async-start(s8[13107200]{0:T(1024)(128)(4,1)} %bitcast.164), calls=%async_computation.31 | async-start | bytes 8388608
  121.2 12.5 %slice-start.5 = ((s8[13107200]{0:T(1024)(128)(4,1)}), s8[4194304]{0:T(1024)(128)(4,1)S(1)}, s32[]{:S(2)}) async-start(s8[13107200]{0:T(1024)(128)(4,1)} %bitcast.164), calls=%async_computation.32 | async-start | bytes 8388608
  121.2 12.5 %slice-start.6 = ((s8[13107200]{0:T(1024)(128)(4,1)}), s8[4194304]{0:T(1024)(128)(4,1)S(1)}, s32[]{:S(2)}) async-start(s8[13107200]{0:T(1024)(128)(4,1)} %bitcast.164), calls=%async_computation.33 | async-start | bytes 8388608
  146.1 73.9 %reduce-scatter.21.cloned.1.call-start = ((), (), s32[]{:S(2)}) async-start(), calls=%async_computation.17 | async-start | bytes 1228800 | tf_op jit(solution)/shard_map/reduce_scatter | solution.py:285
  153.1 66.9 %reduce-scatter.25.cloned.1.call-start = ((), (), s32[]{:S(2)}) async-start(), calls=%async_computation.19 | async-start | bytes 2457600 | tf_op jit(solution)/shard_map/reduce_scatter | solution.py:285
  169.8 51.0 %reduce-scatter.19.cloned.1.call-start = ((), (), s32[]{:S(2)}) async-start(), calls=%async_computation.16 | async-start | bytes 3686400 | tf_op jit(solution)/shard_map/reduce_scatter | solution.py:285
  172.5 12.9 %slice-start.2 = ((s8[13107200]{0:T(1024)(128)(4,1)}), s8[4194304]{0:T(1024)(128)(4,1)S(1)}, s32[]{:S(2)}) async-start(s8[13107200]{0:T(1024)(128)(4,1)} %bitcast.162), calls=%async_computation.29 | async-start | bytes 8388608
  172.5 13.1 %slice-start.3 = ((s8[13107200]{0:T(1024)(128)(4,1)}), s8[524288]{0:T(1024)(128)(4,1)S(1)}, s32[]{:S(2)}) async-start(s8[13107200]{0:T(1024)(128)(4,1)} %bitcast.162), calls=%async_computation.30 | async-start | bytes 1048576
  202.8 28.7 %reduce-scatter.33.cloned.1.call-start = ((), (), s32[]{:S(2)}) async-start(), calls=%async_computation.23 | async-start | bytes 5898240 | tf_op jit(solution)/shard_map/reduce_scatter | solution.py:285
  211.4 35.5 %reduce-scatter.29.cloned.1.call-start = ((), (), s32[]{:S(2)}) async-start(), calls=%async_computation.21 | async-start | bytes 5898240 | tf_op jit(solution)/shard_map/reduce_scatter | solution.py:285
  219.9 162.0 %all-reduce.7.cloned.1.call-start = ((), (), s32[]{:S(2)}) async-start(), calls=%async_computation.26 | async-start | bytes 4096000
  220.7 241.6 %reduce-scatter.35.cloned.1.call-start = ((), (), s32[]{:S(2)}) async-start(), calls=%async_computation.24 | async-start | bytes 1392640
  223.3 368.5 %reduce-scatter.37.cloned.1.call-start = ((), (), s32[]{:S(2)}) async-start(), calls=%async_computation.25 | async-start | bytes 2506752
  235.7 487.9 %reduce-scatter.31.cloned.1.call-start = ((), (), s32[]{:S(2)}) async-start(), calls=%async_computation.22 | async-start | bytes 2088960 | tf_op jit(solution)/shard_map/reduce_scatter | solution.py:287
  255.8 8.9 %all-to-all-start.2 = ((f32[640,2,320]{0,2,1:T(8,128)}), f32[640,2,320]{0,2,1:T(8,128)}, u32[]{:S(2)}, u32[]{:S(2)}) async-start(f32[640,2,320]{0,2,1:T(8,128)} %bitcast.198), calls=%async_computation.2 | async-start | bytes 3276800 | tf_op jit(solution)/shard_map/all_to_all | solution.py:53
  264.7 14.2 %all-to-all-start.5 = ((bf16[640,2,320]{0,2,1:T(8,128)(2,1)}), bf16[640,2,320]{0,2,1:T(8,128)(2,1)S(1)}, u32[]{:S(2)}, u32[]{:S(2)}) async-start(bf16[640,2,320]{0,2,1:T(8,128)(2,1)} %bitcast.202), calls=%async_computation.5 | async-start | bytes 1638400 | tf_op jit(solution)/shard_map/all_to_all | solution.py:53
  278.9 7.3 all-to-all-start.4
  (57 other events, 269.9 us)
Sparse Core Ops, SparseCore 0:
  118.7 11.1 reduce-scatter.26
  146.2 11.1 reduce-scatter.22
  159.7 9.4 reduce-scatter.20
  171.9 10.2 reduce-scatter.24
  203.0 13.2 reduce-scatter.18
  218.4 13.0 reduce-scatter.32
  233.8 13.0 reduce-scatter.28
  253.9 128.0 all-reduce.6
  384.2 77.9 reduce-scatter.34
  467.0 124.7 reduce-scatter.36
  597.4 126.1 reduce-scatter.30
where the time goes:
time: 742 us; the launch traced here: 732 us
  waiting for transfers between devices  402 us (54%)
  matrix products  145 us (20%)
  local copies, waits for them, and re-layouts  58 us (8%)
  blocking collectives  44.6 us (6%)
  other arithmetic  38.3 us (5%)
  starting transfers between devices  27.4 us (4%)
  between operations  16.2 us (2%)
    unnamed x14, waiting for transfers between devices  252 us
    reduce_scatter x1, waiting for transfers between devices, per_device(): lax.psum_scatter(pair, 'dp', scatter_dimension=0, tiled=True)  130 us
    psum x1, blocking collectives, per_device(): lax.psum(jnp.concatenate([gain_local, shift_local], axis=0), ('dp', 'feat'))  40.8 us
    unnamed x141, local copies, waits for them, and re-layouts  30 us
    dot_general x7, matrix products, backward_product(): lax.dot_general(grad, weight, (((1,), (1,)), ((), ())), preferred_element...  28.6 us
    dot_general x7, matrix products, inner(): lax.dot_general(left, right, (((0,), (0,)), ((), ())), preferred_element_...  28.2 us
    dot_general x2, matrix products, attend_backward(): jnp.einsum('qhd,khd->hqk', grad_heads, split_heads(values), preferred_ele...  24.6 us
    reduce_scatter x7, waiting for transfers between devices, per_device(): lax.psum_scatter(term.astype(jnp.bfloat16), 'feat', scatter_dimension=1,...  19.4 us
  transfers between devices with their start and end apart: 17, of which 7 were waited for; matrix products, arithmetic and copies ran while one was open for 23% of the time, Pallas kernels for 0%

commit v1 on v0

--- a/solution.py
+++ b/solution.py
@@ -7,6 +7,11 @@
 HEADS = 8
 EPSILON = 1e-05
 MASKED_SCORE = -1e30
+
+
+def _obtain_teams(mine, axis_tag):
+    arr_now = lax.all_gather(mine, axis_tag)
+    return jnp.sum(arr_now, 0)
 
 
 def as_sent(array):
@@ -267,7 +272,7 @@
     input_grad = grad_mid_one + part_one
     gain_local = jnp.stack([gain_one, gain_two, gain_three], axis=0)
     shift_local = jnp.stack([shift_one, shift_two, shift_three], axis=0)
-    vectors = lax.psum(jnp.concatenate([gain_local, shift_local], axis=0), ("dp", "feat"))
+    vectors = _obtain_teams(jnp.concatenate([gain_local, shift_local], axis=0), ("dp", "feat"))
     half = vectors.shape[1] // lax.axis_size("feat")
     vectors = lax.dynamic_slice_in_dim(vectors, lax.axis_index("feat") * half, half, axis=1)
     gain_grad, shift_grad = (vectors[:3], vectors[3:])

time: 742 us -> 742 us (level)
    all_gather x0 -> x1, blocking collectives: none -> 43.9 us  [_obtain_teams(): arr_now = lax.all_gather(mine, axis_tag)]
    psum x1 -> x0, blocking collectives: 40.8 us -> none  [per_device(): lax.psum(jnp.concatenate([gain_local, shift_local], axis=0), ('dp', 'feat'))]
where the time goes in v1:
time: 742 us; the launch traced here: 732 us
  waiting for transfers between devices  399 us (54%)
  matrix products  145 us (20%)
  local copies, waits for them, and re-layouts  58 us (8%)
  blocking collectives  47.7 us (6%)
  other arithmetic  38.3 us (5%)
  starting transfers between devices  27.4 us (4%)
  between operations  16.2 us (2%)
    unnamed x14, waiting for transfers between devices  249 us
    reduce_scatter x1, waiting for transfers between devices, per_device(): lax.psum_scatter(pair, 'dp', scatter_dimension=0, tiled=True)  130 us
    all_gather x1, blocking collectives, _obtain_teams(): arr_now = lax.all_gather(mine, axis_tag)  43.9 us
    unnamed x141, local copies, waits for them, and re-layouts  30 us
    dot_general x7, matrix products, backward_product(): lax.dot_general(grad, weight, (((1,), (1,)), ((), ())), preferred_element...  28.6 us
    dot_general x7, matrix products, inner(): lax.dot_general(left, right, (((0,), (0,)), ((), ())), preferred_element_...  28.2 us
    dot_general x2, matrix products, attend_backward(): jnp.einsum('qhd,khd->hqk', grad_heads, split_heads(values), preferred_ele...  24.6 us
    reduce_scatter x7, waiting for transfers between devices, per_device(): lax.psum_scatter(term.astype(jnp.bfloat16), 'feat', scatter_dimension=1,...  19.4 us
  transfers between devices with their start and end apart: 17, of which 7 were waited for; matrix products, arithmetic and copies ran while one was open for 23% of the time, Pallas kernels for 0%

profile of v1, /device:TPU:0, one launch (start us, length us, event | category | flops | bytes accessed | tf_op | source)
XLA Modules:
  0.0 732.3 jit_solution(11777765707293187693)
XLA Ops:
  23.2 4.7 all-to-all-start
  38.0 4.7 all-to-all-start.3
  58.6 8.8 %fusion.79 = f32[640,3072]{1,0:T(8,128)} fusion(bf16[640,640]{0,1:T(8,128)(2,1)S(1)} %fusion.60, bf16[3072,640]{1,0:T(8,128)(2,1)} %param.27), kind=kOutput, calls=%fused_computation.178 | convolution fusion | flops 2516582400 | bytes 12615680 | tf_op jit(solution)/shard_map/dot_general | solution.py:32
  97.4 12.5 %fusion.7 = (bf16[640,3072]{1,0:T(8,128)(2,1)S(1)}, bf16[640,3072]{1,0:T(8,128)(2,1)}) fusion(f32[640,3072]{1,0:T(8,128)} %fusion.79, bf16[640,3072]{1,0:T(8,128)(2,1)S(1)} %copy-done.50, f32[640,640]{0,1:T(8,128)S(1)} %get-tuple-element.118, f32[640]{0:T(1024)S(1)} %get-tuple-element.91, f32[640]{0:T(1024)S(1)} %get-tuple-element.130, ...), kind=kOutput, calls=%fused_computation.24 | convolution fusion | flops 2561884160 | bytes 21309440 | tf_op jit(solution)/shard_map/dot_general | solution.py:223
  121.3 12.5 %multiply_reduce_fusion.1 = (f32[8,640]{1,0:T(8,128)S(1)}, f32[8,640,640]{1,2,0:T(8,128)}) fusion(f32[8,640,640]{1,2,0:T(8,128)} %copy-done.2, f32[8,640]{1,0:T(8,128)S(1)} %log_add_fusion.1, bf16[640,8,80]{0,2,1:T(8,128)(2,1)S(1)} %bitcast.173, bf16[640,8,80]{0,2,1:T(8,128)(2,1)} %bitcast.187), kind=kOutput, calls=%fused_computation.9 | convolution fusion | flops 534113280 | bytes 27893760 | tf_op jit(solution)/shard_map/qhd,khd->hqk/dot_general | solution.py:126
  133.8 6.6 multiply_convert_fusion.1
  153.2 5.6 multiply_convert_fusion.2
  158.8 7.3 fusion.52
  172.5 12.1 %multiply_reduce_fusion = (f32[8,640]{1,0:T(8,128)S(1)}, f32[8,640,640]{1,2,0:T(8,128)}) fusion(f32[8,640,640]{1,2,0:T(8,128)} %copy-done.1, f32[8,640]{1,0:T(8,128)S(1)} %log_add_fusion, bf16[640,8,80]{0,2,1:T(8,128)(2,1)S(1)} %bitcast.175, bf16[640,8,80]{0,2,1:T(8,128)(2,1)S(1)} %bitcast.185), kind=kOutput, calls=%fused_computation.6 | convolution fusion | flops 534113280 | bytes 27893760 | tf_op jit(solution)/shard_map/qhd,khd->hqk/dot_general | solution.py:126
  185.6 6.6 multiply_convert_fusion
  204.0 7.4 %convolution_convert_fusion = bf16[3072,640]{0,1:T(8,128)(2,1)} fusion(bf16[640,640]{0,1:T(8,128)(2,1)S(1)} %copy-done.34, bf16[640,3072]{1,0:T(8,128)(2,1)} %get-tuple-element.120), kind=kOutput, calls=%fused_computation.37 | convolution fusion | flops 2538209280 | bytes 8683520 | tf_op jit(solution)/shard_map/dot_general | solution.py:26
  211.5 8.4 %convolution_convert_fusion.1 = bf16[640,3072]{1,0:T(8,128)(2,1)} fusion(bf16[640,3072]{1,0:T(8,128)(2,1)} %copy-done.55, f32[640,640]{0,1:T(8,128)} %copy-done.18, f32[640]{0:T(1024)S(1)} %get-tuple-element.91, f32[640]{0:T(1024)S(1)} %get-tuple-element.130, f32[640]{0:T(1024)S(1)} %get-tuple-element.108, f32[640]{0:T(1024)S(1)} %get-tuple-element.107), kind=kOutput, calls=%fused_computation.38 | convolution fusion | flops 2520596480 | bytes 9512960 | tf_op jit(solution)/shard_map/dot_general | solution.py:26
  223.4 8.2 %reduce-scatter.33.cloned.1.call-done = bf16[3072,320]{0,1:T(8,128)(2,1)} async-done(((bf16[3072,640]{0,1:T(8,128)(2,1)}), bf16[3072,320]{0,1:T(8,128)(2,1)}) %reduce-scatter.33.cloned.1.call-update) | async-done | bytes 1966096 | tf_op jit(solution)/shard_map/reduce_scatter | solution.py:290
  231.6 4.1 copy.180
  235.8 11.1 %reduce-scatter.29.cloned.1.call-done = bf16[640,1536]{1,0:T(8,128)(2,1)} async-done(((bf16[640,3072]{1,0:T(8,128)(2,1)}), bf16[640,1536]{1,0:T(8,128)(2,1)}) %reduce-scatter.29.cloned.1.call-update) | async-done | bytes 1966096 | tf_op jit(solution)/shard_map/reduce_scatter | solution.py:290
  246.9 8.8 %convert_add_fusion.1 = f32[640,640]{0,1:T(8,128)} fusion(f32[640,640]{0,1:T(8,128)} %copy-done.18, bf16[3072,640]{1,0:T(8,128)(2,1)} %param.27, f32[640]{0:T(1024)S(1)} %fusion.61, bf16[640,3072]{1,0:T(8,128)(2,1)} %get-tuple-element.120), kind=kOutput, calls=%fused_computation.93 | convolution fusion | flops 2537881600 | bytes 11143680 | tf_op jit(solution)/shard_map/dot_general | solution.py:226
  255.8 4.8 all-to-all-start.2
  260.6 4.1 convolution_convert_fusion.7
  278.9 4.7 all-to-all-start.4
  289.0 43.9 %all-gather.3 = f32[32,6,640]{2,1,0:T(8,128)S(1)} all-gather(f32[1,6,640]{2,1,0:T(8,128)S(1)} %bitcast.212), channel_id=2, replica_groups=mesh['dp'=16,'feat'=2] {'dp','feat'}, dimensions={0}, use_global_device_ids=true | all-gather | bytes 506880 | tf_op jit(solution)/shard_map/all_gather | solution.py:13
  334.9 47.1 %all-reduce.7.cloned.1.call-done = (bf16[640,320]{0,1:T(8,128)(2,1)}, bf16[640,320]{0,1:T(8,128)(2,1)}, bf16[640,640]{0,1:T(8,128)(2,1)}, bf16[640,320]{0,1:T(8,128)(2,1)}) async-done(((bf16[640,320]{0,1:T(8,128)(2,1)}, bf16[640,320]{0,1:T(8,128)(2,1)}, bf16[640,640]{0,1:T(8,128)(2,1)}, bf16[640,320]{0,1:T(8,128)(2,1)}), (bf16[640,320]{0,1:T(8,128)(2,1)}, bf16[640,320]{0,1:T(8,128)(2,1)}, ...) | async-done | bytes 2048016
  389.1 73.2 %reduce-scatter.35.cloned.1.call-done = bf16[40,960]{1,0:T(8,128)(2,1)} async-done(((bf16[640,960]{1,0:T(8,128)(2,1)}), bf16[40,960]{1,0:T(8,128)(2,1)}) %reduce-scatter.35.cloned.1.call-update) | async-done | bytes 76816
  464.2 127.7 %reduce-scatter.37.cloned.1.call-done = bf16[192,320]{1,0:T(8,128)(2,1)} async-done(((bf16[3072,320]{1,0:T(8,128)(2,1)}), bf16[192,320]{1,0:T(8,128)(2,1)}) %reduce-scatter.37.cloned.1.call-update) | async-done | bytes 122896
  593.7 129.9 %reduce-scatter.31.cloned.1.call-done = bf16[40,1536]{1,0:T(8,128)(2,1)} async-done(((bf16[640,1536]{1,0:T(8,128)(2,1)}), bf16[40,1536]{1,0:T(8,128)(2,1)}) %reduce-scatter.31.cloned.1.call-update) | async-done | bytes 122896 | tf_op jit(solution)/shard_map/reduce_scatter | solution.py:292
  (262 shorter events, 151.5 us)
Async XLA Ops:
  7.2 40.5 %copy-start = (bf16[640,1920]{1,0:T(8,128)(2,1)S(1)}, bf16[640,1920]{1,0:T(8,128)(2,1)}, u32[]{:S(2)}) copy-start(bf16[640,1920]{1,0:T(8,128)(2,1)} %param.21) | copy-start | bytes 7372804
  9.5 13.7 %all-to-all-start.1 = ((bf16[2,640,320]{1,2,0:T(8,128)(2,1)}), bf16[2,640,320]{1,2,0:T(8,128)(2,1)S(1)}, u32[]{:S(2)}, u32[]{:S(2)}) async-start(bf16[2,640,320]{1,2,0:T(8,128)(2,1)} %bitcast.162), calls=%async_computation.1 | async-start | bytes 1638400 | tf_op jit(solution)/shard_map/all_to_all | solution.py:54
  23.2 14.9 %all-to-all-start = ((f32[2,640,320]{1,2,0:T(8,128)}), f32[2,640,320]{1,2,0:T(8,128)}, u32[]{:S(2)}, u32[]{:S(2)}) async-start(f32[2,640,320]{1,2,0:T(8,128)} %bitcast.178), calls=%async_computation | async-start | bytes 3276800 | tf_op jit(solution)/shard_map/all_to_all | solution.py:54
  38.0 19.0 %all-to-all-start.3 = ((f32[2,640,320]{1,2,0:T(8,128)}), f32[2,640,320]{1,2,0:T(8,128)}, u32[]{:S(2)}, u32[]{:S(2)}) async-start(f32[2,640,320]{1,2,0:T(8,128)} %bitcast.177), calls=%async_computation.3 | async-start | bytes 3276800 | tf_op jit(solution)/shard_map/all_to_all | solution.py:54
  42.7 177.3 %reduce-scatter.27.cloned.1.call-start = ((), (), s32[]{:S(2)}) async-start(), calls=%async_computation.20 | async-start | bytes 1228800 | tf_op jit(solution)/shard_map/reduce_scatter | solution.py:290
  96.4 17.2 %copy-start.18 = (f32[640,640]{0,1:T(8,128)}, f32[640,640]{0,1:T(8,128)S(1)}, u32[]{:S(2)}) copy-start(f32[640,640]{0,1:T(8,128)S(1)} %get-tuple-element.118) | copy-start | bytes 4915204
  118.6 101.5 %reduce-scatter.23.cloned.1.call-start = ((), (), s32[]{:S(2)}) async-start(), calls=%async_computation.18 | async-start | bytes 1228800 | tf_op jit(solution)/shard_map/reduce_scatter | solution.py:290
  121.2 12.6 %slice-start.4 = ((s8[13107200]{0:T(1024)(128)(4,1)}), s8[4194304]{0:T(1024)(128)(4,1)S(1)}, s32[]{:S(2)}) async-start(s8[13107200]{0:T(1024)(128)(4,1)} %bitcast.165), calls=%async_computation.31 | async-start | bytes 8388608
  121.2 12.5 %slice-start.5 = ((s8[13107200]{0:T(1024)(128)(4,1)}), s8[4194304]{0:T(1024)(128)(4,1)S(1)}, s32[]{:S(2)}) async-start(s8[13107200]{0:T(1024)(128)(4,1)} %bitcast.165), calls=%async_computation.32 | async-start | bytes 8388608
  146.1 73.9 %reduce-scatter.21.cloned.1.call-start = ((), (), s32[]{:S(2)}) async-start(), calls=%async_computation.17 | async-start | bytes 1228800 | tf_op jit(solution)/shard_map/reduce_scatter | solution.py:290
  153.1 66.9 %reduce-scatter.25.cloned.1.call-start = ((), (), s32[]{:S(2)}) async-start(), calls=%async_computation.19 | async-start | bytes 2457600 | tf_op jit(solution)/shard_map/reduce_scatter | solution.py:290
  169.8 51.0 %reduce-scatter.19.cloned.1.call-start = ((), (), s32[]{:S(2)}) async-start(), calls=%async_computation.16 | async-start | bytes 3686400 | tf_op jit(solution)/shard_map/reduce_scatter | solution.py:290
  172.5 12.9 %slice-start.2 = ((s8[13107200]{0:T(1024)(128)(4,1)}), s8[4194304]{0:T(1024)(128)(4,1)S(1)}, s32[]{:S(2)}) async-start(s8[13107200]{0:T(1024)(128)(4,1)} %bitcast.163), calls=%async_computation.29 | async-start | bytes 8388608
  172.5 13.1 %slice-start.3 = ((s8[13107200]{0:T(1024)(128)(4,1)}), s8[524288]{0:T(1024)(128)(4,1)S(1)}, s32[]{:S(2)}) async-start(s8[13107200]{0:T(1024)(128)(4,1)} %bitcast.163), calls=%async_computation.30 | async-start | bytes 1048576
  202.8 28.7 %reduce-scatter.33.cloned.1.call-start = ((), (), s32[]{:S(2)}) async-start(), calls=%async_computation.23 | async-start | bytes 5898240 | tf_op jit(solution)/shard_map/reduce_scatter | solution.py:290
  211.4 35.5 %reduce-scatter.29.cloned.1.call-start = ((), (), s32[]{:S(2)}) async-start(), calls=%async_computation.21 | async-start | bytes 5898240 | tf_op jit(solution)/shard_map/reduce_scatter | solution.py:290
  219.9 162.1 %all-reduce.7.cloned.1.call-start = ((), (), s32[]{:S(2)}) async-start(), calls=%async_computation.26 | async-start | bytes 4096000
  220.7 241.6 %reduce-scatter.35.cloned.1.call-start = ((), (), s32[]{:S(2)}) async-start(), calls=%async_computation.24 | async-start | bytes 1392640
  223.3 368.6 %reduce-scatter.37.cloned.1.call-start = ((), (), s32[]{:S(2)}) async-start(), calls=%async_computation.25 | async-start | bytes 2506752
  235.7 487.9 %reduce-scatter.31.cloned.1.call-start = ((), (), s32[]{:S(2)}) async-start(), calls=%async_computation.22 | async-start | bytes 2088960 | tf_op jit(solution)/shard_map/reduce_scatter | solution.py:292
  255.8 8.9 %all-to-all-start.2 = ((f32[640,2,320]{0,2,1:T(8,128)}), f32[640,2,320]{0,2,1:T(8,128)}, u32[]{:S(2)}, u32[]{:S(2)}) async-start(f32[640,2,320]{0,2,1:T(8,128)} %bitcast.199), calls=%async_computation.2 | async-start | bytes 3276800 | tf_op jit(solution)/shard_map/all_to_all | solution.py:58
  264.7 14.2 %all-to-all-start.5 = ((bf16[640,2,320]{0,2,1:T(8,128)(2,1)}), bf16[640,2,320]{0,2,1:T(8,128)(2,1)S(1)}, u32[]{:S(2)}, u32[]{:S(2)}) async-start(bf16[640,2,320]{0,2,1:T(8,128)(2,1)} %bitcast.203), calls=%async_computation.5 | async-start | bytes 1638400 | tf_op jit(solution)/shard_map/all_to_all | solution.py:58
  278.9 7.3 all-to-all-start.4
  285.0 48.0 %copy-start.54 = (u32[32]{0:T(128)S(1)}, u32[32]{0:T(128)}, u32[]{:S(2)}) copy-start(u32[32]{0:T(128)} %constant.54) | copy-start | bytes 388
  (57 other events, 278.5 us)
Sparse Core Ops, SparseCore 0:
  118.7 11.1 reduce-scatter.26
  146.2 11.1 reduce-scatter.22
  159.7 9.4 reduce-scatter.20
  171.9 10.2 reduce-scatter.24
  203.0 13.2 reduce-scatter.18
  218.4 13.0 reduce-scatter.32
  233.8 13.0 reduce-scatter.28
  253.9 128.1 all-reduce.6
  384.3 77.9 reduce-scatter.34
  467.1 124.7 reduce-scatter.36
  597.5 126.1 reduce-scatter.30
